TPU v7x, 1024 devices: a whole 4x4x32 slice. The times are simulated.
1024 devices in a mesh: pair: 128 (over y, z), slab: 8 (over x, core).
Axes of the slice: x: 4, y: 4, z: 32, core: 2. Of those that a mesh axis runs over, the one named last changes fastest.
Arguments:
- amplitudes: bfloat16 [3072, 8, 2048], P(None, 'slab', 'pair'), may hold values from -6 to 6
- ladder_integral: bfloat16 [16384, 16384], P('slab', 'pair'), may hold values from -0.046875 to 0.046875
- tile_mask: int32 [128, 128], P('slab', 'pair'), may hold values 0 or 1
- left_factor: bfloat16 [128, 384, 4096], P(None, 'pair', 'slab'), may hold values from -0.0048828125 to 0.0048828125
- right_factor: float32 [128, 4096, 384], P(None, 'pair'), may hold values from -0.5 to 0.5
Outputs:
- residual: float32 [3072, 16384], P('slab', 'pair')
Inputs may be any that keep to these rules, and one draw needn't show every extreme that they name: `tile_mask`: 1 where a pair of tiles may couple, else 0.
All inputs are finite; a program needn't handle non-finite values. No bound on the sum of `tile_mask` on one device may be relied on, other than what follows from the above.
Results may differ from a plain program's by a relative error of at most 0.0003.
Values may be sent and summed in bfloat16 or wider, within the bound.
A program may use at most 64 MiB of HBM per device.

v0:
```python
import jax
import jax.numpy as jnp
from jax import lax
from jax.sharding import PartitionSpec as P

O = 384
TILE = 128
NA = 4
NI = 8


def per_device(amplitudes, ladder_integral, tile_mask, left_factor, right_factor):
    row_count = amplitudes.shape[0]
    own_cols = amplitudes.shape[2]
    own_block = amplitudes.reshape(row_count, own_cols)
    occ_share = O // lax.axis_size("pair")
    pair_cols = ladder_integral.shape[1]
    tile_keep = jnp.repeat(jnp.repeat(tile_mask, TILE, axis=0), TILE, axis=1).astype(jnp.bfloat16)
    masked_integral = ladder_integral * tile_keep
    ladder = jnp.dot(
        lax.all_gather(own_block, "pair", axis=1, tiled=True),
        masked_integral,
        preferred_element_type=jnp.float32,
    )
    relaid = lax.all_to_all(
        own_block.reshape(NI, O, own_cols), "pair", split_axis=1, concat_axis=2, tiled=True
    )
    slab_virt = relaid.shape[2] // NA
    amps_four = relaid.reshape(NI, occ_share, slab_virt, NA)
    cycle_part = jnp.einsum(
        "ikca,lkc->ial", amps_four, left_factor, preferred_element_type=jnp.float32
    )
    cycle_mix = lax.psum(cycle_part, ("pair", "slab"))
    cycle_full = jnp.einsum(
        "ial,lbj->ijba", cycle_mix, right_factor, precision=lax.Precision.HIGHEST
    )
    cycle_full = cycle_full.reshape(row_count, pair_cols)
    share_rows = row_count // lax.axis_size("slab")
    first_row = lax.axis_index("slab") * share_rows
    cycle_block = lax.dynamic_slice_in_dim(cycle_full, first_row, share_rows, 0)
    summed = lax.psum(ladder, "slab")
    ladder_share = lax.dynamic_slice_in_dim(summed, first_row, share_rows, 0)
    return ladder_share + cycle_block


def solution(mesh):
    return jax.shard_map(
        per_device,
        mesh=mesh,
        in_specs=(
            P(None, "slab", "pair"),
            P("slab", "pair"),
            P("slab", "pair"),
            P(None, "pair", "slab"),
            P(None, "pair", None),
        ),
        out_specs=P("slab", "pair"),
        check_vma=False,
    )
```

profile of v0, /device:TPU:1, one launch (start us, length us, event | category | flops | bytes accessed | tf_op | source)
XLA Modules:
  0.0 498.6 jit_solution(618230781634558337)
XLA Ops:
  6.5 0.0 copy-start
  6.5 0.0 copy-start.2
  6.5 0.0 copy-start.1
  6.5 0.0 all-gather.3.cloned.1.call-start
  6.5 0.7 all-gather.3.cloned.1.call-update
  7.3 0.9 copy.17
  8.2 0.5 copy.9
  8.7 1.4 reshape.33
  10.1 33.8 %all-to-all-start = ((bf16[128,2,192]{2,1,0:T(2,128)(2,1)}), bf16[128,2,192]{2,1,0:T(2,128)(2,1)S(1)}, u32[]{:S(2)}, u32[]{:S(2)}) async-start(bf16[128,2,192]{2,1,0:T(2,128)(2,1)} %reshape.33), calls=%async_computation | async-start | bytes 262144 | tf_op jit(solution)/shard_map/all_to_all | solution.py:25
  43.8 0.0 all-reduce.2.cloned.1.call-start
  43.9 0.0 copy-done.2
  43.9 0.1 broadcast_bitcast_fusion
  44.0 257.6 %all-gather.3.cloned.1.call-done = bf16[3072,1,2048]{0,2,1:T(8,128)(2,1)} async-done(((bf16[3072,1,16]{0,2,1:T(8,128)(2,1)}), bf16[3072,1,2048]{0,2,1:T(8,128)(2,1)}) %all-gather.3.cloned.1.call-update) | async-done | bytes 12582928 | tf_op jit(solution)/shard_map/all_gather | solution.py:21
  301.5 0.0 copy-done.1
  301.5 7.7 %fusion.5 = f32[3072,128]{0,1:T(8,128)} fusion(bf16[3072,1,2048]{0,2,1:T(8,128)(2,1)} %all-gather.3.cloned.1.call-done, bf16[2048,128]{1,0:T(8,128)(2,1)S(1)} %copy-done.1, bf16[2048]{0:T(1024)(128)(2,1)S(1)} %broadcast_bitcast_fusion), kind=kOutput, calls=%fused_computation.5 | convolution fusion | flops 1610874880 | bytes 14684160 | tf_op jit(solution)/shard_map/dot_general | solution.py:20
  309.2 0.0 all-reduce.2.cloned.1.call-update
  309.2 0.0 all-to-all-done
  309.2 0.6 reshape.34
  309.8 0.9 copy.10
  310.7 0.0 copy-done
  310.7 0.5 fusion.13
  311.2 170.1 %psum.15 = f32[8,4,128]{2,0,1:T(8,128)S(1)} all-reduce(f32[8,4,128]{2,0,1:T(8,128)S(1)} %fusion.13), channel_id=1, replica_groups=mesh['pair'=128,'slab'=8] {'pair','slab'}, use_global_device_ids=true, to_apply=%region_1.0 | all-reduce | flops 4096 | bytes 32768 | tf_op jit(solution)/shard_map/psum | solution.py:33
  481.4 8.1 %fusion.10 = f32[8,384,32,4]{1,0,2,3:T(8,128)S(1)} fusion(f32[128,32,384]{2,1,0:T(8,128)} %param.9, f32[8,4,128]{2,0,1:T(8,128)S(1)} %psum.15), kind=kOutput, calls=%fused_computation.8 | convolution fusion | flops 603979776 | bytes 7880704 | tf_op jit(solution)/shard_map/ial,lbj->ijba/dot_general | solution.py:34
  489.5 0.2 copy.12
  489.7 0.3 copy.18
  490.0 0.0 all-reduce.2.cloned.1.call-done
  490.0 1.0 dynamic-slice_add_fusion
  491.0 0.8 copy.13
  (1 shorter events, 0.0 us)
Async XLA Ops:
  6.5 304.2 %copy-start = (bf16[128,3,512]{2,0,1:T(8,128)(2,1)S(1)}, bf16[128,3,512]{2,0,1:T(8,128)(2,1)}, u32[]{:S(2)}) copy-start(bf16[128,3,512]{2,0,1:T(8,128)(2,1)} %param.8) | copy-start | bytes 1179652
  6.5 37.3 %copy-start.2 = (s32[16,1]{0,1:T(1,128)S(1)}, s32[16,1]{0,1:T(1,128)}, u32[]{:S(2)}) copy-start(s32[16,1]{0,1:T(1,128)} %param.7) | copy-start | bytes 196
  6.5 295.0 %copy-start.1 = (bf16[2048,128]{1,0:T(8,128)(2,1)S(1)}, bf16[2048,128]{1,0:T(8,128)(2,1)}, u32[]{:S(2)}) copy-start(bf16[2048,128]{1,0:T(8,128)(2,1)} %param.6) | copy-start | bytes 1572868
  6.5 295.0 %all-gather.3.cloned.1.call-start = ((), (), s32[]{:S(2)}) async-start(), calls=%async_computation.2 | async-start | bytes 12681216 | tf_op jit(solution)/shard_map/all_gather | solution.py:21
  10.1 299.2 %all-to-all-start = ((bf16[128,2,192]{2,1,0:T(2,128)(2,1)}), bf16[128,2,192]{2,1,0:T(2,128)(2,1)S(1)}, u32[]{:S(2)}, u32[]{:S(2)}) async-start(bf16[128,2,192]{2,1,0:T(2,128)(2,1)} %reshape.33), calls=%async_computation | async-start | bytes 262144 | tf_op jit(solution)/shard_map/all_to_all | solution.py:25
  43.8 446.2 %all-reduce.2.cloned.1.call-start = ((), (), s32[]{:S(2)}) async-start(), calls=%async_computation.1 | async-start | bytes 3145728 | tf_op jit(solution)/shard_map/psum | solution.py:41
Sparse Core Ops, SparseCore 0:
  11.5 290.0 all-gather.2
  309.4 106.8 all-reduce.1
where the time goes:
time: 499 us
  waiting for transfers between devices  258 us (52%)
  blocking collectives  170 us (34%)
  starting transfers between devices  33.8 us (7%)
  matrix products  16.4 us (3%)
  between operations  13.5 us (3%)
  local copies, waits for them, and re-layouts  5.57 us (1%)
    all_gather x1, waiting for transfers between devices, per_device(): lax.all_gather(own_block, 'pair', axis=1, tiled=True)  258 us
    psum x1, blocking collectives, per_device(): cycle_mix = lax.psum(cycle_part, ('pair', 'slab'))  170 us
    all_to_all x1, starting transfers between devices, per_device(): lax.all_to_all(own_block.reshape(NI, O, own_cols), 'pair', split_axis=1,...  33.8 us
  transfers between devices with their start and end apart: 3, of which 1 were waited for; matrix products, arithmetic and copies ran while one was open for 4% of the time, Pallas kernels for 0%

commit v1 on v0

v1 whole, which is shorter than its diff:
```python
import jax
import jax.numpy as jnp
from jax import lax
from jax.experimental import pallas as pl
from jax.experimental.pallas import tpu as pltpu
from jax.sharding import PartitionSpec as P

O = 384
NA = 4
NI = 8
NY = 4
NZ = 32
NX = 4
NS = 8
KQ = O // NY // 2
HR = NI * KQ
MESH = pl.DeviceIdType.MESH
F32 = jnp.float32
BF16 = jnp.bfloat16
Z_PHASES = ((1, 3), (4, 3), (16, 1))
Z_SHIFTS = tuple(w * q for w, n in Z_PHASES for q in range(1, n + 1))
DOT0 = (((0,), (0,)), ((), ()))


def kernel(
    t_ref, int_ref, mask_ref, left_ref, lad_ref, mix_ref,
    tg, ig, acc, sib, xin, red, fin, tsel, mixp, mslab, mone, myin, mzsend, mzin,
    ys_send, ys_recv, ig_send, ig_recv, z_send, z_recv, sib_sem, x_send, x_recv, yo_send, yo_recv,
    ms_send, ms_recv, my_send, my_recv, mz_send, mz_recv,
):
    pair = lax.axis_index("pair")
    slab = lax.axis_index("slab")
    y, z = lax.div(pair, NZ), lax.rem(pair, NZ)
    x, c = lax.div(slab, 2), lax.rem(slab, 2)

    def at_y(q):
        return {"pair": lax.rem(y + q, NY) * NZ + z, "slab": slab}

    def at_z(q):
        return {"pair": y * NZ + lax.rem(z + q + NZ, NZ), "slab": slab}

    def at_slab(q):
        return {"pair": pair, "slab": lax.rem(slab + q, NS)}

    def at_x(q):
        return {"pair": pair, "slab": lax.rem(x + q, NX) * 2 + c}

    sibling = {"pair": pair, "slab": slab + 1 - 2 * c}

    def remote(src, dst, send, recv, where):
        return pltpu.make_async_remote_copy(
            src_ref=src, dst_ref=dst, send_sem=send, recv_sem=recv, device_id=where, device_id_type=MESH
        )

    barrier = pltpu.get_barrier_semaphore()
    senders = [at_y(q) for q in range(1, NY)] + [at_z(1)] + [at_z(-q) for q in Z_SHIFTS]
    senders += [at_slab(q) for q in range(1, NS)]
    for where in senders:
        pl.semaphore_signal(barrier, inc=1, device_id=where, device_id_type=MESH)

    for tile in range(16):
        rows = int_ref[tile // 4, (tile % 4) * 8:(tile % 4) * 8 + 8]
        keep = mask_ref[tile].astype(F32)
        ig[tile // 4, (tile % 4) * 8:(tile % 4) * 8 + 8, :, 0:128] = (rows.astype(F32) * keep).astype(BF16)
    acc[...] = jnp.zeros_like(acc)
    mixp[...] = jnp.zeros_like(mixp)

    pl.semaphore_wait(barrier, len(senders))

    def y_copy(q):
        return remote(t_ref.at[lax.rem(y + q, NY)], tg.at[:, y, z], ys_send.at[q - 1], ys_recv.at[q - 1], at_y(q))

    def y_arrived(q):
        return remote(t_ref.at[0], tg.at[:, lax.rem(y + NY - q, NY), z], ys_send.at[q - 1], ys_recv.at[q - 1], at_y(q))

    for q in range(1, NY):
        y_copy(q).start()
    tg[:, y, z] = t_ref[y]

    def ig_copy(n, where):
        slot_src, slot_dst, first, count = ((0, 3, 0, 4), (0, 1, 0, 4), (3, 2, 0, 2), (1, 2, 2, 2))[n]
        return remote(
            ig.at[first:first + count, :, :, slot_src * 128:slot_src * 128 + 128],
            ig.at[first:first + count, :, :, slot_dst * 128:slot_dst * 128 + 128],
            ig_send.at[n], ig_recv.at[n], where,
        )

    ig_copies = [ig_copy(n, at_y(1 if n % 2 == 0 else NY - 1)) for n in range(4)]
    ig_copies[0].start()
    ig_copies[1].start()

    for q in range(1, NY):
        y_arrived(q).wait_recv()

    def z_copy(way, h, step):
        sign = 1 - 2 * way
        slot = lax.rem(z - sign * (step - 1) + NZ, NZ)
        return remote(
            tg.at[h, :, slot], tg.at[h, :, slot], z_send.at[way, h, step], z_recv.at[way, h, step], at_z(sign)
        )

    def z_arrived(way, h, step):
        sign = 1 - 2 * way
        slot = lax.rem(z - sign * step + NZ, NZ)
        return remote(
            tg.at[h, :, slot], tg.at[h, :, slot], z_send.at[way, h, step], z_recv.at[way, h, step], at_z(sign)
        )

    streams = [(way, h) for h in range(2) for way in range(2)]
    for way, h in streams:
        z_copy(way, h, 1).start()

    def forward(step):
        for way, h in streams:
            z_arrived(way, h, step).wait_recv()
            z_copy(way, h, step + 1).start()

    def multiply(first, second):
        rhs = jnp.concatenate([ig[:, first].reshape(64, 512), ig[:, second].reshape(64, 512)], axis=0)
        for h in range(2):
            lhs = jnp.concatenate([tg[h, :, first].reshape(64, HR), tg[h, :, second].reshape(64, HR)], axis=0)
            acc[h] += lax.dot_general(lhs, rhs, DOT0, preferred_element_type=F32).reshape(NX, 2, KQ, 512)

    def unit(distance):
        multiply(lax.rem(z + NZ - distance, NZ), lax.rem(z + distance, NZ))

    @pl.loop(1, 4)
    def _(step):
        forward(step)

    ig_copies[0].wait_recv()
    ig_copies[2].start()
    ig_copies[1].wait_recv()
    ig_copies[3].start()

    @pl.loop(4, 8)
    def _(step):
        forward(step)

    ig_copies[2].wait_recv()
    ig_copies[3].wait_recv()

    @pl.loop(8, 15)
    def _(step):
        forward(step)
        unit(2 * step - 15)
        unit(2 * step - 14)

    for way, h in streams:
        z_arrived(way, h, 15).wait_recv()
    z_copy(0, 0, 16).start()
    z_copy(1, 1, 16).start()
    unit(15)
    z_arrived(0, 0, 16).wait_recv()
    z_arrived(1, 1, 16).wait_recv()
    multiply(z, lax.rem(z + 16, NZ))

    sib_copy = remote(acc.at[:, :, 1 - c], sib, sib_sem.at[0], sib_sem.at[1], sibling)
    sib_copy.start()

    lane = lax.broadcasted_iota(jnp.int32, (HR, 128), 1)
    row = lax.broadcasted_iota(jnp.int32, (HR, 128), 0)
    for h in range(2):
        k_own = 3 * z + (lane >> 3) - KQ * h
        hit = (row == KQ * (lane & 7) + k_own) & (k_own >= 0) & (k_own < KQ) & (lane < 24)
        pick = jnp.where(hit, 1.0, 0.0).astype(BF16)
        got = jnp.dot(tg[h].reshape(2048, HR), pick, preferred_element_type=F32)
        if h == 0:
            tsel[...] = got
        else:
            tsel[...] += got
    for a in range(NA):
        own = tsel[pl.ds(a, 512, stride=NA), :].astype(BF16)
        part = jnp.zeros((8, 128), F32)
        for d in range(3):
            whole = lax.dot_general(own, left_ref[d], (((0,), (1,)), ((), ())), preferred_element_type=F32)
            part += whole[8 * d:8 * d + 8]
        mixp[:, a] = part

    def ms_copy(q):
        return remote(mixp.at[lax.rem(slab + q, NS)], mslab.at[q - 1], ms_send.at[q - 1], ms_recv.at[q - 1], at_slab(q))

    for q in range(1, NS):
        ms_copy(q).start()

    sib_copy.wait()

    def x_copy(q):
        return remote(acc.at[:, lax.rem(x + q, NX), c], xin.at[q - 1], x_send.at[q - 1], x_recv.at[q - 1], at_x(q))

    for q in (2, 1, 3):
        there = lax.rem(x + q, NX)
        acc[:, there, c] = acc[:, there, c] + sib[:, there]
        x_copy(q).start()

    for q in range(1, NS):
        ms_copy(q).wait_recv()
    total = mixp[slab]
    for q in range(1, NS):
        total += mslab[q - 1]
    mone[...] = total

    def my_copy(q):
        return remote(mone, myin.at[q - 1], my_send.at[q - 1], my_recv.at[q - 1], at_y(q))

    for q in range(1, NY):
        my_copy(q).start()
    for q in range(1, NY):
        my_copy(q).wait_recv()
        total += myin[q - 1]

    mz_copies = []
    n = 0
    for phase, (width, count) in enumerate(Z_PHASES):
        mzsend[phase] = total
        for q in range(1, count + 1):
            mz_copies.append(remote(mzsend.at[phase], mzin.at[n], mz_send.at[n], mz_recv.at[n], at_z(width * q)))
            mz_copies[n].start()
            n += 1
        if phase == 1:
            mine = acc[:, x, c] + sib[:, x]
            for q in range(1, NX):
                x_copy(q).wait_recv()
                mine += xin[q - 1]
            red[...] = mine

            def yo_copy(q):
                return remote(
                    red.at[:, :, 128 * q:128 * q + 128], fin.at[y], yo_send.at[q - 1], yo_recv.at[q - 1], at_y(q)
                )

            for q in range(1, NY):
                yo_copy(q).start()
            fin[y] = red[:, :, 0:128]
        for k in range(n - count, n):
            mz_copies[k].wait_recv()
            total += mzin[k]
    mix_ref[...] = total

    for q in range(1, NY):
        remote(
            red.at[:, :, 128 * q:128 * q + 128], fin.at[lax.rem(y + NY - q, NY)],
            yo_send.at[q - 1], yo_recv.at[q - 1], at_y(q),
        ).wait_recv()
    lad_ref[...] = fin[...]

    for q in range(1, NY):
        y_copy(q).wait_send()
        my_copy(q).wait_send()
        yo_copy(q).wait_send()
    for copy in ig_copies:
        copy.wait_send()
    for way, h in streams:
        @pl.loop(1, 16)
        def _(step):
            z_copy(way, h, step).wait_send()
    z_copy(0, 0, 16).wait_send()
    z_copy(1, 1, 16).wait_send()
    for q in range(1, NX):
        x_copy(q).wait_send()
    for q in range(1, NS):
        ms_copy(q).wait_send()
    for copy in mz_copies:
        copy.wait_send()


def per_device(amplitudes, ladder_integral, tile_mask, left_factor, right_factor):
    own = amplitudes.reshape(NI, NY, 2, KQ, 16)
    relaid = jnp.transpose(own, (1, 2, 4, 0, 3)).reshape(NY, 2, 16, HR)
    integral = ladder_integral.reshape(NY, NZ, 16, 128)
    left = jnp.transpose(left_factor, (1, 0, 2))
    vmem = pl.BlockSpec(memory_space=pltpu.VMEM)
    dma = pltpu.SemaphoreType.DMA
    n_mz = len(Z_SHIFTS)
    ladder, mix = pl.pallas_call(
        kernel,
        out_shape=(
            jax.ShapeDtypeStruct((NY, 2, KQ, 128), F32),
            jax.ShapeDtypeStruct((8, 128), F32),
        ),
        in_specs=[vmem, vmem, pl.BlockSpec(memory_space=pltpu.SMEM), vmem],
        out_specs=(vmem, vmem),
        scratch_shapes=[
            pltpu.VMEM((2, NY, NZ, 16, HR), BF16),
            pltpu.VMEM((NY, NZ, 16, 512), BF16),
            pltpu.VMEM((2, NX, 2, KQ, 512), F32),
            pltpu.VMEM((2, NX, KQ, 512), F32),
            pltpu.VMEM((NX - 1, 2, KQ, 512), F32),
            pltpu.VMEM((2, KQ, 512), F32),
            pltpu.VMEM((NY, 2, KQ, 128), F32),
            pltpu.VMEM((2048, 128), F32),
            pltpu.VMEM((NS, 8, 128), F32),
            pltpu.VMEM((NS - 1, 8, 128), F32),
            pltpu.VMEM((8, 128), F32),
            pltpu.VMEM((NY - 1, 8, 128), F32),
            pltpu.VMEM((len(Z_PHASES), 8, 128), F32),
            pltpu.VMEM((n_mz, 8, 128), F32),
            dma((NY - 1,)), dma((NY - 1,)),
            dma((4,)), dma((4,)),
            dma((2, 2, 17)), dma((2, 2, 17)),
            dma((2,)),
            dma((NX - 1,)), dma((NX - 1,)),
            dma((NY - 1,)), dma((NY - 1,)),
            dma((NS - 1,)), dma((NS - 1,)),
            dma((NY - 1,)), dma((NY - 1,)),
            dma((n_mz,)), dma((n_mz,)),
        ],
        compiler_params=pltpu.CompilerParams(
            collective_id=0, has_side_effects=True, vmem_limit_bytes=40 * 1024 * 1024
        ),
    )(relaid, integral, tile_mask.reshape(16), left)
    cycle = jnp.einsum("al,lbj->jba", mix[:NA], right_factor, precision=lax.Precision.HIGHEST)
    return ladder.reshape(O, 128) + cycle.reshape(O, 128)


def solution(mesh):
    return jax.shard_map(
        per_device,
        mesh=mesh,
        in_specs=(
            P(None, "slab", "pair"),
            P("slab", "pair"),
            P("slab", "pair"),
            P(None, "pair", "slab"),
            P(None, "pair", None),
        ),
        out_specs=P("slab", "pair"),
        check_vma=False,
    )
```

time: 499 us -> 142 us (0.28)
  waiting for transfers between devices: 258 us -> 0 us
  blocking collectives: 170 us -> 0 us
  Pallas kernels: 0 us -> 127 us
  starting transfers between devices: 33.8 us -> 0 us
  between operations: 13.5 us -> 0.06 us
  matrix products: 16.4 us -> 7.79 us
    all_gather x1 -> x0, waiting for transfers between devices: 258 us -> none  [per_device(): lax.all_gather(own_block, 'pair', axis=1, tiled=True)]
    psum x1 -> x0, blocking collectives: 170 us -> none  [per_device(): cycle_mix = lax.psum(cycle_part, ('pair', 'slab'))]
    pallas_call x0 -> x1, Pallas kernels: none -> 127 us  [per_device(): pl.pallas_call(kernel, out_shape=(jax.ShapeDtypeStruct((NY, 2, KQ, 128),...]
    all_to_all x1 -> x0, starting transfers between devices: 33.8 us -> none  [per_device(): lax.all_to_all(own_block.reshape(NI, O, own_cols), 'pair', split_axis=1,...]
    dot_general x3 -> x1, matrix products: 16.4 us -> 7.79 us  [per_device(): jnp.einsum('al,lbj->jba', mix[:NA], right_factor, precision=lax.Precision...]
  transfers between devices with their start and end apart: 3 -> 0, of which waited for: 1 -> 0; matrix products, arithmetic and copies ran while one was open for 4% -> 0% of each run, Pallas kernels for 0% -> 0%
where the time goes in v1:
time: 142 us; the launch traced here: 140 us
  Pallas kernels  127 us (89%)
  matrix products  7.79 us (5%)
  local copies, waits for them, and re-layouts  4.28 us (3%)
    pallas_call x1, Pallas kernels, per_device(): pl.pallas_call(kernel, out_shape=(jax.ShapeDtypeStruct((NY, 2, KQ, 128),...  127 us
    dot_general x1, matrix products, per_device(): jnp.einsum('al,lbj->jba', mix[:NA], right_factor, precision=lax.Precision...  7.79 us

profile of v1, /device:TPU:1, one launch (start us, length us, event | category | flops | bytes accessed | tf_op | source)
XLA Modules:
  0.0 139.8 jit_solution(15534441934258008412)
XLA Ops:
  0.0 1.2 reshape.18
  1.2 0.2 reshape.19.t_ref
  1.4 0.0 copy-start
  1.4 1.0 copy-done
  2.5 0.0 copy-start.1
  2.5 1.0 copy-done.1
  3.5 0.0 copy-start.2
  3.5 0.7 copy-done.2
  4.1 127.0 %shard_map.55 = (f32[4,2,48,128]{3,2,1,0:T(8,128)S(1)}, f32[8,128]{1,0:T(8,128)S(1)}) custom-call(bf16[4,2,16,384]{3,2,1,0:T(8,128)(2,1)S(1)} %reshape.19.t_ref, bf16[4,32,16,128]{3,2,1,0:T(8,128)(2,1)S(1)} %bitcast.19, s32[16]{0:T(128)S(1)} %bitcast.21, bf16[3,128,512]{2,1,0:T(8,128)(2,1)S(1)} %bitcast.20), custom_call_target="tpu_custom_call" | custom-call | tf_op jit(solution)/shard_map/pallas_call | solution.py:275
  131.1 7.8 %fusion.2 = f32[384,32,4]{0,2,1:T(4,128)S(1)} fusion(f32[128,32,384]{2,1,0:T(8,128)} %param.9, f32[8,128]{1,0:T(8,128)S(1)} %get-tuple-element.8), kind=kOutput, calls=%fused_computation.2 | convolution fusion | flops 75497472 | bytes 6490112 | tf_op jit(solution)/shard_map/al,lbj->jba/dot_general | solution.py:312
  138.9 0.1 reshape.23
  139.0 0.1 copy.8
  139.1 0.7 bitcast_add_fusion
  (1 shorter events, 0.0 us)
Async XLA Ops:
  1.4 1.0 copy-start
  2.5 1.0 copy-start.1
  3.5 0.7 copy-start.2

commit v2 on v1

v2 whole, which is shorter than its diff:
```python
import jax
import jax.numpy as jnp
from jax import lax
from jax.experimental import pallas as pl
from jax.experimental.pallas import tpu as pltpu
from jax.sharding import PartitionSpec as P

O = 384
NA = 4
NI = 8
NY = 4
NZ = 32
NX = 4
NS = 8
KQ = O // NY // 2
HR = NI * KQ
MESH = pl.DeviceIdType.MESH
F32 = jnp.float32
BF16 = jnp.bfloat16
Z_PHASES = ((-3, -2, -1, 1, 2, 3, 4), (-12, -4, 4, 12))
L_PART = 8
DOT0 = (((0,), (0,)), ((), ()))


def kernel(
    t_ref, int_hbm, mask_ref, left_hbm, right_hbm, out_ref,
    int_ref, left_ref, right_ref, tsend, tg, ig, acc, sib, xin, red, fin, tsel, mixp, mslab, mone, myin, mzsend, mzin,
    rt_hi, rt_lo, spread,
    in_sem, left_in, ys_send, ys_recv, ig_send, ig_recv, z_send, z_recv, sib_send, sib_recv, x_send, x_recv, yo_send, yo_recv,
    ms_send, ms_recv, my_send, my_recv, mz_send, mz_recv,
):
    pair = lax.axis_index("pair")
    slab = lax.axis_index("slab")
    y, z = lax.div(pair, NZ), lax.rem(pair, NZ)
    x, c = lax.div(slab, 2), lax.rem(slab, 2)

    def at_y(q):
        return {"pair": lax.rem(y + q, NY) * NZ + z, "slab": slab}

    def at_z(q):
        return {"pair": y * NZ + lax.rem(z + q + NZ, NZ), "slab": slab}

    def at_slab(q):
        return {"pair": pair, "slab": lax.rem(slab + q, NS)}

    def at_x(q):
        return {"pair": pair, "slab": lax.rem(x + q, NX) * 2 + c}

    sibling = {"pair": pair, "slab": slab + 1 - 2 * c}

    def remote(src, dst, send, recv, where):
        return pltpu.make_async_remote_copy(
            src_ref=src, dst_ref=dst, send_sem=send, recv_sem=recv, device_id=where, device_id_type=MESH
        )

    loads = [
        pltpu.make_async_copy(here, there, in_sem.at[n])
        for n, (here, there) in enumerate(((int_hbm, int_ref), (left_hbm, left_ref), (right_hbm, right_ref)))
    ]
    for load in loads:
        load.start()

    barrier = pltpu.get_barrier_semaphore()
    senders = [at_y(q) for q in range(1, NY)] + [at_slab(q) for q in range(1, NS)] + [at_z(-1)]
    for where in senders:
        pl.semaphore_signal(barrier, inc=1, device_id=where, device_id_type=MESH)

    for there in range(NY):
        for h in range(2):
            first = (2 * there + h) * KQ
            tsend[there, h] = jnp.concatenate([t_ref[:, i * O + first:i * O + first + KQ] for i in range(NI)], axis=1)

    pl.semaphore_wait(barrier, len(senders))

    def y_copy(q):
        return remote(tsend.at[lax.rem(y + q, NY)], tg.at[:, y, z], ys_send.at[q - 1], ys_recv.at[q - 1], at_y(q))

    def y_arrived(q):
        return remote(tsend.at[0], tg.at[:, lax.rem(y + NY - q, NY), z], ys_send.at[q - 1], ys_recv.at[q - 1], at_y(q))

    for q in (2, 1, 3):
        y_copy(q).start()
    pl.semaphore_signal(left_in, inc=1, device_id=at_z(1), device_id_type=MESH)
    tg[:, y, z] = tsend[y]

    loads[0].wait()
    for tile in range(16):
        rows = int_ref[tile // 4, (tile % 4) * 8:(tile % 4) * 8 + 8]
        keep = mask_ref[tile].astype(F32)
        ig[tile // 4, (tile % 4) * 8:(tile % 4) * 8 + 8, :, 0:128] = (rows.astype(F32) * keep).astype(BF16)
    acc[...] = jnp.zeros_like(acc)
    mixp[...] = jnp.zeros_like(mixp)

    def ig_copy(n, where):
        slot_src, slot_dst, first, count = ((0, 3, 0, 4), (0, 1, 0, 4), (3, 2, 0, 2), (1, 2, 2, 2))[n]
        return remote(
            ig.at[first:first + count, :, :, slot_src * 128:slot_src * 128 + 128],
            ig.at[first:first + count, :, :, slot_dst * 128:slot_dst * 128 + 128],
            ig_send.at[n], ig_recv.at[n], where,
        )

    ig_copies = [ig_copy(n, at_y(1 if n % 2 == 0 else NY - 1)) for n in range(4)]
    ig_copies[0].start()
    ig_copies[1].start()

    for q in range(1, NY):
        y_arrived(q).wait_recv()

    def z_copy(stream, step, arrived=False):
        way, h, part = stream
        sign = 1 - 2 * way
        slot = lax.rem(z - sign * (step - (0 if arrived else 1)) + NZ, NZ)
        piece = tg.at[h, 2 * part:2 * part + 2, slot]
        return remote(piece, piece, z_send.at[way, h, part, step], z_recv.at[way, h, part, step], at_z(sign))

    streams = [(way, h, part) for h in range(2) for part in range(2) for way in range(2)]
    for stream in streams:
        if stream[0] == 0:
            z_copy(stream, 1).start()
    pl.semaphore_wait(left_in, 1)
    for stream in streams:
        if stream[0] == 1:
            z_copy(stream, 1).start()

    def forward(step):
        for stream in streams:
            z_copy(stream, step, True).wait_recv()
            z_copy(stream, step + 1).start()

    def split(part):
        wide = right_ref[pl.ds(part * L_PART, L_PART)].reshape(L_PART * 32, O).T
        high = wide.astype(BF16)
        where = pl.ds(pl.multiple_of(part * L_PART * 32, L_PART * 32), L_PART * 32)
        rt_hi[:, where] = high
        rt_lo[:, where] = (wide - high.astype(F32)).astype(BF16)

    loads[1].wait()
    loads[2].wait()

    def multiply(first, second):
        rhs = jnp.concatenate([ig[:, first].reshape(64, 512), ig[:, second].reshape(64, 512)], axis=0)
        for h in range(2):
            lhs = jnp.concatenate([tg[h, :, first].reshape(64, HR), tg[h, :, second].reshape(64, HR)], axis=0)
            acc[h] += lax.dot_general(lhs, rhs, DOT0, preferred_element_type=F32).reshape(NX, 2, KQ, 512)

    def unit(distance):
        multiply(lax.rem(z + NZ - distance, NZ), lax.rem(z + distance, NZ))

    @pl.loop(1, 4)
    def _(step):
        forward(step)
        split(2 * step - 2)
        split(2 * step - 1)

    ig_copies[0].wait_recv()
    ig_copies[2].start()
    ig_copies[1].wait_recv()
    ig_copies[3].start()

    @pl.loop(4, 8)
    def _(step):
        forward(step)
        split(2 * step - 2)
        split(2 * step - 1)

    split(14)
    split(15)
    ig_copies[2].wait_recv()
    ig_copies[3].wait_recv()

    @pl.loop(8, 15)
    def _(step):
        forward(step)
        unit(2 * step - 15)
        unit(2 * step - 14)

    last = [stream for stream in streams if stream[0] == stream[1]]
    for stream in streams:
        z_copy(stream, 15, True).wait_recv()
        if stream in last:
            z_copy(stream, 16).start()
    unit(15)
    for stream in last:
        z_copy(stream, 16, True).wait_recv()
    multiply(z, lax.rem(z + 16, NZ))

    sib_copies = [remote(acc.at[h, :, 1 - c], sib.at[h], sib_send.at[h], sib_recv.at[h], sibling) for h in range(2)]
    for copy in sib_copies:
        copy.start()

    lane = lax.broadcasted_iota(jnp.int32, (HR, 128), 1)
    row = lax.broadcasted_iota(jnp.int32, (HR, 128), 0)
    for h in range(2):
        k_own = 3 * z + (lane >> 3) - KQ * h
        hit = (row == KQ * (lane & 7) + k_own) & (k_own >= 0) & (k_own < KQ) & (lane < 24)
        pick = jnp.where(hit, 1.0, 0.0).astype(BF16)
        got = jnp.dot(tg[h].reshape(2048, HR), pick, preferred_element_type=F32)
        if h == 0:
            tsel[...] = got
        else:
            tsel[...] += got
    for a in range(NA):
        own = tsel[pl.ds(a, 512, stride=NA), :].astype(BF16)
        part = jnp.zeros((8, 128), F32)
        for d in range(3):
            whole = lax.dot_general(own, left_ref[d], (((0,), (1,)), ((), ())), preferred_element_type=F32)
            part += whole[8 * d:8 * d + 8]
        mixp[:, a] = part

    def ms_copy(q):
        return remote(mixp.at[lax.rem(slab + q, NS)], mslab.at[q - 1], ms_send.at[q - 1], ms_recv.at[q - 1], at_slab(q))

    for q in range(1, NS):
        ms_copy(q).start()

    def x_copy(h, q):
        there = lax.rem(x + q, NX)
        return remote(acc.at[h, there, c], xin.at[q - 1, h], x_send.at[h, q - 1], x_recv.at[h, q - 1], at_x(q))

    for h in range(2):
        sib_copies[h].wait()
        for q in (2, 1, 3):
            there = lax.rem(x + q, NX)
            acc[h, there, c] = acc[h, there, c] + sib[h, there]
            x_copy(h, q).start()

    for q in range(1, NS):
        ms_copy(q).wait_recv()
    total = mixp[slab]
    for q in range(1, NS):
        total += mslab[q - 1]
    mone[...] = total

    def my_copy(q):
        return remote(mone, myin.at[q - 1], my_send.at[q - 1], my_recv.at[q - 1], at_y(q))

    for q in range(1, NY):
        my_copy(q).start()
    for q in range(1, NY):
        my_copy(q).wait_recv()
        total += myin[q - 1]

    def mz_copy(n):
        phase = 0 if n < len(Z_PHASES[0]) else 1
        return remote(mzsend.at[phase], mzin.at[n], mz_send.at[n], mz_recv.at[n], at_z(sum(Z_PHASES, ())[n]))

    def yo_copy(q):
        return remote(red.at[:, :, 128 * q:128 * q + 128], fin.at[y], yo_send.at[q - 1], yo_recv.at[q - 1], at_y(q))

    near, far = range(len(Z_PHASES[0])), range(len(Z_PHASES[0]), len(Z_PHASES[0]) + len(Z_PHASES[1]))
    mzsend[0] = total
    for n in near:
        mz_copy(n).start()
    for n in near:
        mz_copy(n).wait_recv()
        total += mzin[n]
    mzsend[1] = total
    for n in far:
        mz_copy(n).start()

    for h in range(2):
        mine = acc[h, x, c] + sib[h, x]
        for q in range(1, NX):
            x_copy(h, q).wait_recv()
            mine += xin[q - 1, h]
        red[h] = mine
    for q in (2, 1, 3):
        yo_copy(q).start()
    fin[y] = red[:, :, 0:128]

    total = jnp.zeros_like(total)
    for n in far:
        mz_copy(n).wait_recv()
        total += mzin[n]

    lane8 = lax.broadcasted_iota(jnp.int32, (8, 128), 1)
    row8 = lax.broadcasted_iota(jnp.int32, (8, 128), 0)
    put = jnp.where((lane8 & (NA - 1)) == row8, 1.0, 0.0)
    by_l = lax.dot_general(total, put, DOT0, precision=lax.Precision.HIGHEST, preferred_element_type=F32)
    high = by_l.astype(BF16).astype(F32)
    lane32 = lax.broadcasted_iota(jnp.int32, (128, 32, 128), 2)
    row32 = lax.broadcasted_iota(jnp.int32, (128, 32, 128), 1)
    on_diagonal = (lane32 >> 2) == row32
    for n, term in enumerate((high, by_l - high)):
        wide = jnp.where(on_diagonal, jnp.broadcast_to(term[:, None, :], (128, 32, 128)), 0.0)
        spread[:, 128 * n:128 * n + 128] = wide.reshape(4096, 128).astype(BF16)
    both = jnp.dot(rt_hi[...], spread[...], preferred_element_type=F32)
    cycle = both[:, 0:128] + both[:, 128:256]
    cycle += jnp.dot(rt_lo[...], spread[:, 0:128], preferred_element_type=F32)

    for q in range(1, NY):
        remote(
            red.at[:, :, 128 * q:128 * q + 128], fin.at[lax.rem(y + NY - q, NY)],
            yo_send.at[q - 1], yo_recv.at[q - 1], at_y(q),
        ).wait_recv()
    out_ref[...] = fin[...].reshape(O, 128) + cycle

    for q in range(1, NY):
        y_copy(q).wait_send()
        my_copy(q).wait_send()
        yo_copy(q).wait_send()
    for copy in ig_copies:
        copy.wait_send()
    for stream in streams:
        @pl.loop(1, 16)
        def _(step):
            z_copy(stream, step).wait_send()
    for stream in last:
        z_copy(stream, 16).wait_send()
    for h in range(2):
        for q in range(1, NX):
            x_copy(h, q).wait_send()
    for q in range(1, NS):
        ms_copy(q).wait_send()
    for n in range(len(near) + len(far)):
        mz_copy(n).wait_send()


def per_device(amplitudes, ladder_integral, tile_mask, left_factor, right_factor):
    own = amplitudes.reshape(NI * O, 16).T
    integral = ladder_integral.reshape(NY, NZ, 16, 128)
    left = jnp.transpose(left_factor, (1, 0, 2))
    vmem = pl.BlockSpec(memory_space=pltpu.VMEM)
    anywhere = pl.BlockSpec(memory_space=pl.ANY)
    dma = pltpu.SemaphoreType.DMA
    n_mz = sum(len(phase) for phase in Z_PHASES)
    return pl.pallas_call(
        kernel,
        out_shape=jax.ShapeDtypeStruct((O, 128), F32),
        in_specs=[vmem, anywhere, pl.BlockSpec(memory_space=pltpu.SMEM), anywhere, anywhere],
        out_specs=vmem,
        scratch_shapes=[
            pltpu.VMEM((NY, NZ, 16, 128), BF16),
            pltpu.VMEM((3, 128, 512), BF16),
            pltpu.VMEM((128, 32, O), F32),
            pltpu.VMEM((NY, 2, 16, HR), BF16),
            pltpu.VMEM((2, NY, NZ, 16, HR), BF16),
            pltpu.VMEM((NY, NZ, 16, 512), BF16),
            pltpu.VMEM((2, NX, 2, KQ, 512), F32),
            pltpu.VMEM((2, NX, KQ, 512), F32),
            pltpu.VMEM((NX - 1, 2, KQ, 512), F32),
            pltpu.VMEM((2, KQ, 512), F32),
            pltpu.VMEM((NY, 2, KQ, 128), F32),
            pltpu.VMEM((2048, 128), F32),
            pltpu.VMEM((NS, 8, 128), F32),
            pltpu.VMEM((NS - 1, 8, 128), F32),
            pltpu.VMEM((8, 128), F32),
            pltpu.VMEM((NY - 1, 8, 128), F32),
            pltpu.VMEM((2, 8, 128), F32),
            pltpu.VMEM((n_mz, 8, 128), F32),
            pltpu.VMEM((O, 4096), BF16),
            pltpu.VMEM((O, 4096), BF16),
            pltpu.VMEM((4096, 256), BF16),
            dma((3,)),
            pltpu.SemaphoreType.REGULAR,
            dma((NY - 1,)), dma((NY - 1,)),
            dma((4,)), dma((4,)),
            dma((2, 2, 2, 17)), dma((2, 2, 2, 17)),
            dma((2,)), dma((2,)),
            dma((2, NX - 1)), dma((2, NX - 1)),
            dma((NY - 1,)), dma((NY - 1,)),
            dma((NS - 1,)), dma((NS - 1,)),
            dma((NY - 1,)), dma((NY - 1,)),
            dma((n_mz,)), dma((n_mz,)),
        ],
        compiler_params=pltpu.CompilerParams(
            collective_id=0, has_side_effects=True, vmem_limit_bytes=48 * 1024 * 1024
        ),
    )(own, integral, tile_mask.reshape(16), left, right_factor)


def solution(mesh):
    return jax.shard_map(
        per_device,
        mesh=mesh,
        in_specs=(
            P(None, "slab", "pair"),
            P("slab", "pair"),
            P("slab", "pair"),
            P(None, "pair", "slab"),
            P(None, "pair", None),
        ),
        out_specs=P("slab", "pair"),
        check_vma=False,
    )
```

time: 142 us -> 114 us (0.80); the launches traced: 140 us -> 114 us
  Pallas kernels: 127 us -> 109 us
  matrix products: 7.79 us -> 0 us
    pallas_call x1, Pallas kernels: 127 us -> 109 us  [per_device(): pl.pallas_call(kernel, out_shape=jax.ShapeDtypeStruct((O, 128), F32), in_...]
    dot_general x1 -> x0, matrix products: 7.79 us -> none  [per_device(): jnp.einsum('al,lbj->jba', mix[:NA], right_factor, precision=lax.Precision...]
    reshape x5 -> x0, local copies, waits for them, and re-layouts: 1.59 us -> none  [the longest x2 1.21 us: per_device(): own = amplitudes.reshape(NI, NY, 2, KQ, 16)]
    unnamed x6 -> x9, local copies, waits for them, and re-layouts: 2.69 us -> 4.26 us
where the time goes in v2:
time: 114 us
  Pallas kernels  109 us (96%)
  local copies, waits for them, and re-layouts  4.26 us (4%)
    pallas_call x1, Pallas kernels, per_device(): pl.pallas_call(kernel, out_shape=jax.ShapeDtypeStruct((O, 128), F32), in_...  109 us
    unnamed x9, local copies, waits for them, and re-layouts  4.26 us

profile of v2, /device:TPU:1, one launch (start us, length us, event | category | flops | bytes accessed | tf_op | source)
XLA Modules:
  0.0 113.5 jit_solution(17397733854630951568)
XLA Ops:
  0.0 0.0 copy-start
  0.0 1.0 copy-done
  1.0 0.0 copy-start.1
  1.0 1.0 copy-done.1
  2.0 0.0 copy-start.2
  2.0 0.9 copy-done.2
  2.9 0.0 copy-start.3
  2.9 0.7 copy-done.3
  3.6 109.2 %shard_map.55 = f32[384,128]{1,0:T(8,128)S(1)} custom-call(bf16[16,3072]{1,0:T(8,128)(2,1)S(1)} %bitcast.8, bf16[4,32,16,128]{3,2,1,0:T(8,128)(2,1)S(1)} %bitcast.6, s32[16]{0:T(128)S(1)} %bitcast.9, bf16[3,128,512]{2,1,0:T(8,128)(2,1)S(1)} %bitcast.7, f32[128,32,384]{2,1,0:T(8,128)} %right_hbm.1), custom_call_target="tpu_custom_call" | custom-call | tf_op jit(solution)/shard_map/pallas_call | solution.py:327
  112.8 0.7 copy.7
Async XLA Ops:
  0.0 1.0 copy-start
  1.0 1.0 copy-start.1
  2.0 0.9 copy-start.2
  2.9 0.7 copy-start.3

commit v3 on v2

--- a/solution.py
+++ b/solution.py
@@ -23,10 +23,10 @@
 
 
 def kernel(
-    t_ref, int_hbm, mask_ref, left_hbm, right_hbm, out_ref,
-    int_ref, left_ref, right_ref, tsend, tg, ig, acc, sib, xin, red, fin, tsel, mixp, mslab, mone, myin, mzsend, mzin,
+    t_hbm, int_hbm, mask_ref, left_hbm, right_hbm, out_ref,
+    t_ref, int_ref, left_ref, right_ref, tsend, tg, ig, acc, sib, xin, red, fin, rsel, msg, rx, rxf, mixp, mslab, mone, myin, mzsend, mzin,
     rt_hi, rt_lo, spread,
-    in_sem, left_in, ys_send, ys_recv, ig_send, ig_recv, z_send, z_recv, sib_send, sib_recv, x_send, x_recv, yo_send, yo_recv,
+    in_sem, left_in, known, ma_send, ma_recv, ys_send, ys_recv, ig_send, ig_recv, z_send, z_recv, sib_send, sib_recv, x_send, x_recv, yo_send, yo_recv,
     ms_send, ms_recv, my_send, my_recv, mz_send, mz_recv,
 ):
     pair = lax.axis_index("pair")
@@ -55,7 +55,7 @@
 
     loads = [
         pltpu.make_async_copy(here, there, in_sem.at[n])
-        for n, (here, there) in enumerate(((int_hbm, int_ref), (left_hbm, left_ref), (right_hbm, right_ref)))
+        for n, (here, there) in enumerate(((t_hbm, t_ref), (int_hbm, int_ref), (left_hbm, left_ref), (right_hbm, right_ref)))
     ]
     for load in loads:
         load.start()
@@ -65,6 +65,7 @@
     for where in senders:
         pl.semaphore_signal(barrier, inc=1, device_id=where, device_id_type=MESH)
 
+    loads[0].wait()
     for there in range(NY):
         for h in range(2):
             first = (2 * there + h) * KQ
@@ -83,7 +84,7 @@
     pl.semaphore_signal(left_in, inc=1, device_id=at_z(1), device_id_type=MESH)
     tg[:, y, z] = tsend[y]
 
-    loads[0].wait()
+    loads[1].wait()
     for tile in range(16):
         rows = int_ref[tile // 4, (tile % 4) * 8:(tile % 4) * 8 + 8]
         keep = mask_ref[tile].astype(F32)
@@ -122,6 +123,45 @@
         if stream[0] == 1:
             z_copy(stream, 1).start()
 
+    def tell(n):
+        for q in (-(1 << n), 1 << n):
+            pl.semaphore_signal(known.at[n], inc=1, device_id=at_z(q), device_id_type=MESH)
+
+    def learn(n):
+        pl.semaphore_wait(known.at[n], 2)
+
+    tell(0)
+
+    lane = lax.broadcasted_iota(jnp.int32, (HR, 512), 1)
+    row = lax.broadcasted_iota(jnp.int32, (HR, 512), 0)
+    d_of = (lane >> 3) & 3
+    pick = jnp.where((row == KQ * (lane & 7) + 3 * (lane >> 5) + d_of) & (d_of < 3), 1.0, 0.0).astype(BF16)
+    got = jnp.dot(tg[:, :, z].reshape(128, HR), pick, preferred_element_type=F32)
+    for group in range(4):
+        rsel[group] = got[:, 128 * group:128 * group + 128]
+    quarter = lax.broadcasted_iota(jnp.int32, (16, 128), 1) >> 5
+
+    @pl.loop(0, 8)
+    def _(g):
+        h, group = lax.div(g, 4), lax.rem(g, 4)
+        own = [rsel[group, pl.ds(pl.multiple_of(h * 64 + there * 16, 16), 16)] for there in range(NY)]
+        for zz in range(4):
+            put = jnp.zeros((16, 128), F32)
+            for there in range(NY):
+                shift = (there - zz) % 4 * 32
+                moved = pltpu.roll(own[there], shift, 1) if shift else own[there]
+                put = jnp.where(quarter == there, moved, put)
+            msg[4 * g + zz] = put.astype(BF16)
+
+    rx[z] = msg[z]
+
+    def ma_copy(q):
+        return remote(msg.at[lax.rem(z + q, NZ)], rx.at[z], ma_send.at[q - 1], ma_recv.at[q - 1], at_z(q))
+
+    def ma_arrived(q):
+        here = rx.at[lax.rem(z + NZ - q, NZ)]
+        return remote(here, here, ma_send.at[q - 1], ma_recv.at[q - 1], at_z(q))
+
     def forward(step):
         for stream in streams:
             z_copy(stream, step, True).wait_recv()
@@ -134,8 +174,8 @@
         rt_hi[:, where] = high
         rt_lo[:, where] = (wide - high.astype(F32)).astype(BF16)
 
-    loads[1].wait()
     loads[2].wait()
+    loads[3].wait()
 
     def multiply(first, second):
         rhs = jnp.concatenate([ig[:, first].reshape(64, 512), ig[:, second].reshape(64, 512)], axis=0)
@@ -146,39 +186,115 @@
     def unit(distance):
         multiply(lax.rem(z + NZ - distance, NZ), lax.rem(z + distance, NZ))
 
-    @pl.loop(1, 4)
-    def _(step):
-        forward(step)
+    def splits(step):
         split(2 * step - 2)
         split(2 * step - 1)
 
+    forward(1)
+    learn(0)
+    tell(1)
+    splits(1)
+    forward(2)
+    learn(1)
+    tell(2)
+    splits(2)
+    forward(3)
+    splits(3)
     ig_copies[0].wait_recv()
     ig_copies[2].start()
     ig_copies[1].wait_recv()
     ig_copies[3].start()
-
-    @pl.loop(4, 8)
-    def _(step):
+    forward(4)
+    learn(2)
+    tell(3)
+    splits(4)
+    forward(5)
+    splits(5)
+
+    order = [16 + (1 - 2 * (n % 2)) * ((n + 1) // 2) for n in range(NZ - 1)]
+    for step in (6, 7):
         forward(step)
-        split(2 * step - 2)
-        split(2 * step - 1)
-
+        if step == 6:
+            learn(3)
+        for q in order[8 * (step - 6):8 * (step - 5)]:
+            ma_copy(q).start()
+        splits(step)
     split(14)
     split(15)
     ig_copies[2].wait_recv()
     ig_copies[3].wait_recv()
 
-    @pl.loop(8, 15)
+    def units(step):
+        unit(2 * step - 15)
+        unit(2 * step - 14)
+
+    for step in (8, 9):
+        forward(step)
+        for q in order[8 * (step - 6):8 * (step - 5)]:
+            ma_copy(q).start()
+        units(step)
+
+    @pl.loop(10, 12)
     def _(step):
         forward(step)
-        unit(2 * step - 15)
-        unit(2 * step - 14)
+        units(step)
+
+    forward(12)
+
+    @pl.loop(1, NZ)
+    def _(q):
+        ma_arrived(q).wait_recv()
+
+    rxf[...] = rx[...].astype(F32).reshape(512, 128)
+    blocks = [(d, there) for d in range(3) for there in range(NY)]
+    factor = jnp.concatenate([left_ref[d, :, 128 * there:128 * there + 128] for d, there in blocks], axis=0)
+    for a in range(NA):
+        own = rxf[pl.ds(a, 128, stride=NA), :].astype(BF16)
+        whole = lax.dot_general(own, factor, (((0,), (1,)), ((), ())), preferred_element_type=F32)
+        part = jnp.zeros((8, 128), F32)
+        for n, (d, there) in enumerate(blocks):
+            part += whole[32 * there + 8 * d:32 * there + 8 * d + 8, 128 * n:128 * n + 128]
+        mixp[:, a] = part
+
+    def ms_copy(q):
+        return remote(mixp.at[lax.rem(slab + q, NS)], mslab.at[q - 1], ms_send.at[q - 1], ms_recv.at[q - 1], at_slab(q))
+
+    for q in range(1, NS):
+        ms_copy(q).start()
+    units(12)
+    forward(13)
+    units(13)
+    forward(14)
+    total = mixp[slab]
+    for q in range(1, NS):
+        ms_copy(q).wait_recv()
+        total += mslab[q - 1]
+    mone[...] = total
+
+    def my_copy(q):
+        return remote(mone, myin.at[q - 1], my_send.at[q - 1], my_recv.at[q - 1], at_y(q))
+
+    for q in (2, 1, 3):
+        my_copy(q).start()
+    units(14)
 
     last = [stream for stream in streams if stream[0] == stream[1]]
     for stream in streams:
         z_copy(stream, 15, True).wait_recv()
         if stream in last:
             z_copy(stream, 16).start()
+
+    def mz_copy(n):
+        phase = 0 if n < len(Z_PHASES[0]) else 1
+        return remote(mzsend.at[phase], mzin.at[n], mz_send.at[n], mz_recv.at[n], at_z(sum(Z_PHASES, ())[n]))
+
+    near, far = range(len(Z_PHASES[0])), range(len(Z_PHASES[0]), len(Z_PHASES[0]) + len(Z_PHASES[1]))
+    for q in range(1, NY):
+        my_copy(q).wait_recv()
+        total += myin[q - 1]
+    mzsend[0] = total
+    for n in near:
+        mz_copy(n).start()
     unit(15)
     for stream in last:
         z_copy(stream, 16, True).wait_recv()
@@ -188,30 +304,12 @@
     for copy in sib_copies:
         copy.start()
 
-    lane = lax.broadcasted_iota(jnp.int32, (HR, 128), 1)
-    row = lax.broadcasted_iota(jnp.int32, (HR, 128), 0)
-    for h in range(2):
-        k_own = 3 * z + (lane >> 3) - KQ * h
-        hit = (row == KQ * (lane & 7) + k_own) & (k_own >= 0) & (k_own < KQ) & (lane < 24)
-        pick = jnp.where(hit, 1.0, 0.0).astype(BF16)
-        got = jnp.dot(tg[h].reshape(2048, HR), pick, preferred_element_type=F32)
-        if h == 0:
-            tsel[...] = got
-        else:
-            tsel[...] += got
-    for a in range(NA):
-        own = tsel[pl.ds(a, 512, stride=NA), :].astype(BF16)
-        part = jnp.zeros((8, 128), F32)
-        for d in range(3):
-            whole = lax.dot_general(own, left_ref[d], (((0,), (1,)), ((), ())), preferred_element_type=F32)
-            part += whole[8 * d:8 * d + 8]
-        mixp[:, a] = part
-
-    def ms_copy(q):
-        return remote(mixp.at[lax.rem(slab + q, NS)], mslab.at[q - 1], ms_send.at[q - 1], ms_recv.at[q - 1], at_slab(q))
-
-    for q in range(1, NS):
-        ms_copy(q).start()
+    for n in near:
+        mz_copy(n).wait_recv()
+        total += mzin[n]
+    mzsend[1] = total
+    for n in far:
+        mz_copy(n).start()
 
     def x_copy(h, q):
         there = lax.rem(x + q, NX)
@@ -224,39 +322,10 @@
             acc[h, there, c] = acc[h, there, c] + sib[h, there]
             x_copy(h, q).start()
 
-    for q in range(1, NS):
-        ms_copy(q).wait_recv()
-    total = mixp[slab]
-    for q in range(1, NS):
-        total += mslab[q - 1]
-    mone[...] = total
-
-    def my_copy(q):
-        return remote(mone, myin.at[q - 1], my_send.at[q - 1], my_recv.at[q - 1], at_y(q))
-
-    for q in range(1, NY):
-        my_copy(q).start()
-    for q in range(1, NY):
-        my_copy(q).wait_recv()
-        total += myin[q - 1]
-
-    def mz_copy(n):
-        phase = 0 if n < len(Z_PHASES[0]) else 1
-        return remote(mzsend.at[phase], mzin.at[n], mz_send.at[n], mz_recv.at[n], at_z(sum(Z_PHASES, ())[n]))
-
-    def yo_copy(q):
-        return remote(red.at[:, :, 128 * q:128 * q + 128], fin.at[y], yo_send.at[q - 1], yo_recv.at[q - 1], at_y(q))
-
-    near, far = range(len(Z_PHASES[0])), range(len(Z_PHASES[0]), len(Z_PHASES[0]) + len(Z_PHASES[1]))
-    mzsend[0] = total
-    for n in near:
-        mz_copy(n).start()
-    for n in near:
-        mz_copy(n).wait_recv()
-        total += mzin[n]
-    mzsend[1] = total
-    for n in far:
-        mz_copy(n).start()
+    def yo_copy(h, q, src_y):
+        return remote(
+            red.at[h, :, 128 * q:128 * q + 128], fin.at[src_y, h], yo_send.at[h, q - 1], yo_recv.at[h, q - 1], at_y(q)
+        )
 
     for h in range(2):
         mine = acc[h, x, c] + sib[h, x]
@@ -264,9 +333,9 @@
             x_copy(h, q).wait_recv()
             mine += xin[q - 1, h]
         red[h] = mine
-    for q in (2, 1, 3):
-        yo_copy(q).start()
-    fin[y] = red[:, :, 0:128]
+        for q in (2, 1, 3):
+            yo_copy(h, q, y).start()
+        fin[y, h] = mine[:, 0:128]
 
     total = jnp.zeros_like(total)
     for n in far:
@@ -288,17 +357,16 @@
     cycle = both[:, 0:128] + both[:, 128:256]
     cycle += jnp.dot(rt_lo[...], spread[:, 0:128], preferred_element_type=F32)
 
-    for q in range(1, NY):
-        remote(
-            red.at[:, :, 128 * q:128 * q + 128], fin.at[lax.rem(y + NY - q, NY)],
-            yo_send.at[q - 1], yo_recv.at[q - 1], at_y(q),
-        ).wait_recv()
+    for h in range(2):
+        for q in range(1, NY):
+            yo_copy(h, q, lax.rem(y + NY - q, NY)).wait_recv()
     out_ref[...] = fin[...].reshape(O, 128) + cycle
 
     for q in range(1, NY):
         y_copy(q).wait_send()
         my_copy(q).wait_send()
-        yo_copy(q).wait_send()
+        for h in range(2):
+            yo_copy(h, q, y).wait_send()
     for copy in ig_copies:
         copy.wait_send()
     for stream in streams:
@@ -315,21 +383,26 @@
     for n in range(len(near) + len(far)):
         mz_copy(n).wait_send()
 
+    @pl.loop(1, NZ)
+    def _(q):
+        ma_copy(q).wait_send()
+
 
 def per_device(amplitudes, ladder_integral, tile_mask, left_factor, right_factor):
     own = amplitudes.reshape(NI * O, 16).T
     integral = ladder_integral.reshape(NY, NZ, 16, 128)
     left = jnp.transpose(left_factor, (1, 0, 2))
     vmem = pl.BlockSpec(memory_space=pltpu.VMEM)
-    anywhere = pl.BlockSpec(memory_space=pl.ANY)
+    hbm = pl.BlockSpec(memory_space=pltpu.HBM)
     dma = pltpu.SemaphoreType.DMA
     n_mz = sum(len(phase) for phase in Z_PHASES)
     return pl.pallas_call(
         kernel,
         out_shape=jax.ShapeDtypeStruct((O, 128), F32),
-        in_specs=[vmem, anywhere, pl.BlockSpec(memory_space=pltpu.SMEM), anywhere, anywhere],
+        in_specs=[hbm, hbm, pl.BlockSpec(memory_space=pltpu.SMEM), hbm, hbm],
         out_specs=vmem,
         scratch_shapes=[
+            pltpu.VMEM((16, NI * O), BF16),
             pltpu.VMEM((NY, NZ, 16, 128), BF16),
             pltpu.VMEM((3, 128, 512), BF16),
             pltpu.VMEM((128, 32, O), F32),
@@ -341,7 +414,10 @@
             pltpu.VMEM((NX - 1, 2, KQ, 512), F32),
             pltpu.VMEM((2, KQ, 512), F32),
             pltpu.VMEM((NY, 2, KQ, 128), F32),
-            pltpu.VMEM((2048, 128), F32),
+            pltpu.VMEM((4, 128, 128), F32),
+            pltpu.VMEM((NZ, 16, 128), BF16),
+            pltpu.VMEM((NZ, 16, 128), BF16),
+            pltpu.VMEM((512, 128), F32),
             pltpu.VMEM((NS, 8, 128), F32),
             pltpu.VMEM((NS - 1, 8, 128), F32),
             pltpu.VMEM((8, 128), F32),
@@ -351,20 +427,22 @@
             pltpu.VMEM((O, 4096), BF16),
             pltpu.VMEM((O, 4096), BF16),
             pltpu.VMEM((4096, 256), BF16),
-            dma((3,)),
+            dma((4,)),
             pltpu.SemaphoreType.REGULAR,
+            pltpu.SemaphoreType.REGULAR((4,)),
+            dma((NZ - 1,)), dma((NZ - 1,)),
             dma((NY - 1,)), dma((NY - 1,)),
             dma((4,)), dma((4,)),
             dma((2, 2, 2, 17)), dma((2, 2, 2, 17)),
             dma((2,)), dma((2,)),
             dma((2, NX - 1)), dma((2, NX - 1)),
-            dma((NY - 1,)), dma((NY - 1,)),
+            dma((2, NY - 1)), dma((2, NY - 1)),
             dma((NS - 1,)), dma((NS - 1,)),
             dma((NY - 1,)), dma((NY - 1,)),
             dma((n_mz,)), dma((n_mz,)),
         ],
         compiler_params=pltpu.CompilerParams(
-            collective_id=0, has_side_effects=True, vmem_limit_bytes=48 * 1024 * 1024
+            collective_id=0, has_side_effects=True, vmem_limit_bytes=60 * 1024 * 1024
         ),
     )(own, integral, tile_mask.reshape(16), left, right_factor)
 

time: 114 us -> 108 us (0.947)
  Pallas kernels: 109 us -> 106 us
  local copies, waits for them, and re-layouts: 4.26 us -> 1.62 us
    pallas_call x1, Pallas kernels: 109 us -> 106 us  [per_device(): pl.pallas_call(kernel, out_shape=jax.ShapeDtypeStruct((O, 128), F32), in_...]
    unnamed x9 -> x1, local copies, waits for them, and re-layouts: 4.26 us -> 1.62 us
where the time goes in v3:
time: 108 us
  Pallas kernels  106 us (98%)
  local copies, waits for them, and re-layouts  1.62 us (2%)
    pallas_call x1, Pallas kernels, per_device(): pl.pallas_call(kernel, out_shape=jax.ShapeDtypeStruct((O, 128), F32), in_...  106 us

profile of v3, /device:TPU:1, one launch (start us, length us, event | category | flops | bytes accessed | tf_op | source)
XLA Modules:
  0.0 107.7 jit_solution(17316084010070180060)
XLA Ops:
  0.0 106.1 %shard_map.55 = f32[384,128]{1,0:T(8,128)} custom-call(bf16[16,3072]{1,0:T(8,128)(2,1)} %bitcast.8, bf16[4,32,16,128]{3,2,1,0:T(8,128)(2,1)} %bitcast.6, s32[16]{0:T(128)} %bitcast.9, bf16[3,128,512]{2,1,0:T(8,128)(2,1)} %bitcast.7, f32[128,32,384]{2,1,0:T(8,128)} %right_hbm.1), custom_call_target="tpu_custom_call" | custom-call | tf_op jit(solution)/shard_map/pallas_call | solution.py:399
  106.1 1.6 %copy.7 = f32[384,128]{1,0:T(8,128)} copy(f32[384,128]{1,0:T(8,128)} %shard_map.55) | data formatting | bytes 393216

commit v4 on v3

v4 whole, which is shorter than its diff:
```python
import jax
import jax.numpy as jnp
from jax import lax
from jax.experimental import pallas as pl
from jax.experimental.pallas import tpu as pltpu
from jax.sharding import PartitionSpec as P

O = 384
NA = 4
NI = 8
NY = 4
NZ = 32
NX = 4
NS = 8
KQ = O // NY // 2
HR = NI * KQ
MESH = pl.DeviceIdType.MESH
F32 = jnp.float32
BF16 = jnp.bfloat16
Z_PHASES = ((-3, -2, -1, 1, 2, 3, 4), (-12, -4, 4, 12))
L_PART = 8
NEAR = 10
FAR = range(NEAR + 1, NZ - NEAR)
DOT0 = (((0,), (0,)), ((), ()))


def kernel(
    t_hbm, int_hbm, mask_ref, left_hbm, right_hbm, lad_ref, cyc_ref,
    t_ref, int_ref, left_ref, right_ref, tsend, tg, ts, ig, acc, sib, xin, red, fin, rsel, msg, rx, rxf,
    tsel, pick_own, mixp, mixq, mslab, mone, myin, mzsend, mzin, mfin, rt_hi, rt_lo, spread,
    in_sem, left_in, known, ys_send, ys_recv, yt_send, yt_recv, ig_send, ig_recv, z_send, z_recv, l_send, l_recv,
    hand_send, hand_recv, ma_send, ma_recv, sib_send, sib_recv, x_send, x_recv, yo_send, yo_recv,
    ms_send, ms_recv, my_send, my_recv, mz_send, mz_recv, far_send, far_recv,
):
    pair = lax.axis_index("pair")
    slab = lax.axis_index("slab")
    y, z = lax.div(pair, NZ), lax.rem(pair, NZ)
    x, c = lax.div(slab, 2), lax.rem(slab, 2)

    def at_y(q, core=None):
        return {"pair": lax.rem(y + q, NY) * NZ + z, "slab": slab if core is None else 2 * x + core}

    def at_z(q):
        return {"pair": y * NZ + lax.rem(z + q + NZ, NZ), "slab": slab}

    def at_slab(q):
        return {"pair": pair, "slab": lax.rem(slab + q, NS)}

    def at_x(q):
        return {"pair": pair, "slab": lax.rem(x + q, NX) * 2 + c}

    sibling = {"pair": pair, "slab": slab + 1 - 2 * c}

    def remote(src, dst, send, recv, where):
        return pltpu.make_async_remote_copy(
            src_ref=src, dst_ref=dst, send_sem=send, recv_sem=recv, device_id=where, device_id_type=MESH
        )

    loads = [
        pltpu.make_async_copy(here, there, in_sem.at[n])
        for n, (here, there) in enumerate(
            ((t_hbm, t_ref), (int_hbm, int_ref), (left_hbm, left_ref.at[c]), (right_hbm, right_ref))
        )
    ]
    for load in loads:
        load.start()

    rx[...] = jnp.zeros_like(rx)

    barrier = pltpu.get_barrier_semaphore()
    senders = [at_y(q) for q in range(1, NY)] + [at_y(q, 1 - c) for q in range(1, NY)]
    senders += [at_slab(q) for q in range(1, NS)] + [at_z(-1), at_z(-2)]
    for where in senders:
        pl.semaphore_signal(barrier, inc=1, device_id=where, device_id_type=MESH)

    loads[0].wait()
    for there in range(NY):
        for h in range(2):
            first = (2 * there + h) * KQ
            tsend[there, h] = jnp.concatenate([t_ref[:, i * O + first:i * O + first + KQ] for i in range(NI)], axis=1)

    pl.semaphore_wait(barrier, len(senders))

    def y_copy(q):
        return remote(tsend.at[lax.rem(y + q, NY)], tg.at[:, y, z], ys_send.at[q - 1], ys_recv.at[q - 1], at_y(q))

    def y_arrived(q):
        return remote(tsend.at[0], tg.at[:, lax.rem(y + NY - q, NY), z], ys_send.at[q - 1], ys_recv.at[q - 1], at_y(q))

    def yt_copy(q):
        return remote(tsend.at[lax.rem(y + q, NY)], ts.at[:, y, z], yt_send.at[q], yt_recv.at[q], at_y(q, 1))

    def yt_arrived(q):
        return remote(tsend.at[0], ts.at[:, lax.rem(y + NY - q, NY), z], yt_send.at[q], yt_recv.at[q], at_y(q, 1))

    @pl.when(c == 0)
    def _():
        for q in (2, 1, 3, 0):
            yt_copy(q).start()

    for q in (2, 1, 3):
        y_copy(q).start()
    for q in (1, 2):
        pl.semaphore_signal(left_in, inc=1, device_id=at_z(q), device_id_type=MESH)
    tg[:, y, z] = tsend[y]

    def tell(n):
        for q in (-(2 << n), 2 << n):
            pl.semaphore_signal(known.at[n], inc=1, device_id=at_z(q), device_id_type=MESH)

    def learn(n):
        pl.semaphore_wait(known.at[n], 2)

    @pl.when(c == 0)
    def _():
        pl.semaphore_wait(left_in, 2)
        tell(0)

    loads[1].wait()
    for tile in range(16):
        rows = int_ref[tile // 4, (tile % 4) * 8:(tile % 4) * 8 + 8]
        keep = mask_ref[tile].astype(F32)
        ig[tile // 4, (tile % 4) * 8:(tile % 4) * 8 + 8, :, 0:128] = (rows.astype(F32) * keep).astype(BF16)

    def ig_copy(n, where):
        slot_src, slot_dst, first, count = ((0, 3, 0, 4), (0, 1, 0, 4), (3, 2, 0, 2), (1, 2, 2, 2))[n]
        return remote(
            ig.at[first:first + count, :, :, slot_src * 128:slot_src * 128 + 128],
            ig.at[first:first + count, :, :, slot_dst * 128:slot_dst * 128 + 128],
            ig_send.at[n], ig_recv.at[n], where,
        )

    ig_copies = [ig_copy(n, at_y(1 if n % 2 == 0 else NY - 1)) for n in range(4)]
    ig_copies[0].start()
    ig_copies[1].start()

    def ig_forward():
        ig_copies[0].wait_recv()
        ig_copies[2].start()
        ig_copies[1].wait_recv()
        ig_copies[3].start()

    def ig_complete():
        ig_copies[2].wait_recv()
        ig_copies[3].wait_recv()

    def z_copy(stream, step, arrived=False):
        way, of, h = stream
        sign = 1 - 2 * way
        slot = lax.rem(z - sign * (step - (0 if arrived else 1)) + NZ, NZ)
        piece = (ts, tg)[of].at[h, :, slot]
        return remote(piece, piece, z_send.at[way, of, h, step], z_recv.at[way, of, h, step], at_z(sign))

    streams = [(way, of, h) for h in range(2) for of in range(2) for way in range(2)]
    last = [stream for stream in streams if stream[0] == stream[2]]

    def l_copy(way, step):
        slot = lax.rem(z - (1 - 2 * way) * step + NZ, NZ)
        return remote(ts.at[:, :, slot], tg.at[:, :, slot], l_send.at[way, step], l_recv.at[way, step], sibling)

    for q in range(1, NY):
        y_arrived(q).wait_recv()

    @pl.when(c == 1)
    def _():
        for q in range(NY):
            yt_arrived(q).wait_recv()
        for stream in streams:
            if stream[0] == 0:
                z_copy(stream, 1).start()

        pl.semaphore_wait(left_in, 2)
        for stream in streams:
            if stream[0] == 1:
                z_copy(stream, 1).start()

    @pl.when(c == 0)
    def _():
        learn(0)
        tell(1)

    acc[...] = jnp.zeros_like(acc)
    mixp[...] = jnp.zeros_like(mixp)

    lane = lax.broadcasted_iota(jnp.int32, (HR, 512), 1)
    row = lax.broadcasted_iota(jnp.int32, (HR, 512), 0)
    d_of = (lane >> 3) & 3
    pick = jnp.where((row == KQ * (lane & 7) + 3 * (lane >> 5) + d_of) & (d_of < 3), 1.0, 0.0).astype(BF16)
    got = jnp.dot(tg[:, :, z].reshape(128, HR), pick, preferred_element_type=F32)
    for group in range(4):
        rsel[group] = got[:, 128 * group:128 * group + 128]
    quarter = lax.broadcasted_iota(jnp.int32, (16, 128), 1) >> 5

    @pl.loop(0, 8)
    def _(g):
        h, group = lax.div(g, 4), lax.rem(g, 4)
        own = [rsel[group, pl.ds(pl.multiple_of(h * 64 + there * 16, 16), 16)] for there in range(NY)]
        for zz in range(4):
            put = jnp.zeros((16, 128), F32)
            for there in range(NY):
                shift = (there - zz) % 4 * 32
                moved = pltpu.roll(own[there], shift, 1) if shift else own[there]
                put = jnp.where(quarter == there, moved, put)
            msg[4 * g + zz, c] = put.astype(BF16)

    hands = [
        remote(msg.at[:, 1], msg.at[:, 1], hand_send.at[0], hand_recv.at[0], sibling),
        remote(left_ref.at[1], left_ref.at[1], hand_send.at[1], hand_recv.at[1], sibling),
        remote(mixp, mixq, hand_send.at[2], hand_recv.at[2], sibling),
    ]
    loads[2].wait()

    @pl.when(c == 1)
    def _():
        hands[0].start()
        hands[1].start()

    def ma_copy(q):
        return remote(msg.at[lax.rem(z + q, NZ)], rx.at[z], ma_send.at[q - 1], ma_recv.at[q - 1], at_z(q))

    def ma_arrived(q):
        here = rx.at[lax.rem(z + NZ - q, NZ)]
        return remote(here, here, ma_send.at[q - 1], ma_recv.at[q - 1], at_z(q))

    def ms_copy(q):
        there = mixp.at[pl.ds(2 * lax.rem(x + q, NX), 2)]
        return remote(there, mslab.at[q - 1], ms_send.at[q - 1], ms_recv.at[q - 1], at_x(q))

    def my_copy(q):
        return remote(mone, myin.at[q - 1], my_send.at[q - 1], my_recv.at[q - 1], at_y(q))

    def mz_copy(n):
        return remote(mzsend.at[0], mzin.at[n], mz_send.at[n], mz_recv.at[n], at_z(Z_PHASES[0][n]))

    def far_copy(n, of):
        there = {"pair": y * NZ + lax.rem(z + Z_PHASES[1][n] + NZ, NZ), "slab": 2 * x + of}
        return remote(mzsend.at[1, of], mfin.at[n], far_send.at[n, of], far_recv.at[n], there)

    near, far = range(len(Z_PHASES[0])), range(len(Z_PHASES[1]))

    def split(part):
        wide = right_ref[pl.ds(part * L_PART, L_PART)].reshape(L_PART * 32, O).T
        high = wide.astype(BF16)
        where = pl.ds(pl.multiple_of(part * L_PART * 32, L_PART * 32), L_PART * 32)
        rt_hi[:, where] = high
        rt_lo[:, where] = (wide - high.astype(F32)).astype(BF16)

    def multiply(first, second):
        rhs = jnp.concatenate([ig[:, first].reshape(64, 512), ig[:, second].reshape(64, 512)], axis=0)
        for h in range(2):
            lhs = jnp.concatenate([tg[h, :, first].reshape(64, HR), tg[h, :, second].reshape(64, HR)], axis=0)
            acc[h] += lax.dot_general(lhs, rhs, DOT0, preferred_element_type=F32).reshape(NX, 2, KQ, 512)

    def unit(distance):
        multiply(lax.rem(z + NZ - distance, NZ), lax.rem(z + distance, NZ))

    tsel[...] = jnp.zeros_like(tsel)
    lane = lax.broadcasted_iota(jnp.int32, (HR, 128), 1)
    row = lax.broadcasted_iota(jnp.int32, (HR, 128), 0)
    for h in range(2):
        k_own = 3 * z + (lane >> 3) - KQ * h
        hit = (row == KQ * (lane & 7) + k_own) & (k_own >= 0) & (k_own < KQ) & (lane < 24)
        pick_own[h] = jnp.where(hit, 1.0, 0.0).astype(BF16)

    def select(slots):
        got = 0.0
        for h in range(2):
            rows = jnp.concatenate([tg[h, :, slot].reshape(64, HR) for slot in slots], axis=0)
            got += jnp.dot(rows, pick_own[h], preferred_element_type=F32)
        for n, slot in enumerate(slots):
            for there in range(NY):
                first = 64 * n + 16 * there
                tsel[pl.ds(pl.multiple_of((there * NZ + slot) * 16, 16), 16)] = got[first:first + 16]

    def select_at(distance):
        select((lax.rem(z + NZ - distance, NZ), lax.rem(z + distance, NZ)))

    def mix_near():
        for a in range(NA):
            own = tsel[pl.ds(a, 512, stride=NA), :].astype(BF16)
            part = mixp[:, a]
            for d in range(3):
                whole = lax.dot_general(own, left_ref[c, d], (((0,), (1,)), ((), ())), preferred_element_type=F32)
                part += whole[8 * d:8 * d + 8]
            mixp[:, a] = part

    select((z,))
    loads[3].wait()

    @pl.when(c == 1)
    def _():
        def forward(step):
            for stream in streams:
                z_copy(stream, step, True).wait_recv()
                z_copy(stream, step + 1).start()
            for way in range(2):
                l_copy(way, step).start()

        def splits(step):
            split(2 * step - 2)
            split(2 * step - 1)

        @pl.loop(1, 4)
        def _(step):
            forward(step)
            select_at(step)
            splits(step)

        ig_forward()

        @pl.loop(4, 8)
        def _(step):
            forward(step)
            select_at(step)
            splits(step)

        split(14)
        split(15)
        ig_complete()

        def units(step):
            unit(2 * step - 15)
            unit(2 * step - 14)

        @pl.loop(8, NEAR)
        def _(step):
            forward(step)
            select_at(step)
            units(step)

        forward(NEAR)
        select_at(NEAR)
        mix_near()
        hands[2].start()
        units(NEAR)

        @pl.loop(NEAR + 1, 15)
        def _(step):
            forward(step)
            units(step)

        for stream in streams:
            z_copy(stream, 15, True).wait_recv()
            if stream in last:
                z_copy(stream, 16).start()
        for way in range(2):
            l_copy(way, 15).start()
        unit(15)
        for stream in last:
            z_copy(stream, 16, True).wait_recv()
        l_copy(0, 16).start()

    @pl.when(c == 0)
    def _():
        def forward(step):
            for way in range(2):
                l_copy(way, step).wait_recv()

        @pl.loop(0, 9)
        def _(part):
            split(part)

        learn(1)
        tell(2)
        ig_forward()

        @pl.loop(9, 16)
        def _(part):
            split(part)

        hands[0].wait_recv()
        learn(2)

        @pl.loop(0, len(FAR))
        def _(n):
            ma_copy(16 + (1 - 2 * lax.rem(n, 2)) * lax.div(n + 1, 2)).start()

        ig_complete()

        @pl.loop(1, NEAR - 1)
        def _(step):
            forward(step)
            select_at(step)
            unit(step)

        @pl.loop(FAR[0], FAR[-1] + 1)
        def _(q):
            ma_arrived(q).wait_recv()

        hands[1].wait_recv()
        rxf[0] = rx[:, 0].astype(F32).reshape(512, 128)
        rxf[1] = rx[:, 1].astype(F32).reshape(512, 128)
        blocks = [(d, there) for d in range(3) for there in range(NY)]

        @pl.loop(0, 2)
        def _(of):
            factor = jnp.concatenate([left_ref[of, d, :, 128 * there:128 * there + 128] for d, there in blocks], axis=0)
            for a in range(NA):
                own = rxf[of, pl.ds(a, 128, stride=NA), :].astype(BF16)
                whole = lax.dot_general(own, factor, (((0,), (1,)), ((), ())), preferred_element_type=F32)
                part = mixp[:, a]
                for n, (d, there) in enumerate(blocks):
                    part += whole[32 * there + 8 * d:32 * there + 8 * d + 8, 128 * n:128 * n + 128]
                mixp[:, a] = part

        for step in (NEAR - 1, NEAR):
            forward(step)
            select_at(step)
        mix_near()
        hands[2].wait_recv()
        mixp[...] += mixq[...]
        for q in (2, 1, 3):
            ms_copy(q).start()
        total = mixp[pl.ds(2 * x, 2)]
        for q in range(1, NX):
            ms_copy(q).wait_recv()
            total += mslab[q - 1]
        mone[...] = total
        for q in (2, 1, 3):
            my_copy(q).start()
        for q in range(1, NY):
            my_copy(q).wait_recv()
            total += myin[q - 1]
        mzsend[0] = total
        for n in near:
            mz_copy(n).start()
        for n in near:
            mz_copy(n).wait_recv()
            total += mzin[n]
        mzsend[1] = total
        for of in (1, 0):
            for n in far:
                far_copy(n, of).start()

        unit(NEAR - 1)
        unit(NEAR)

        @pl.loop(NEAR + 1, 16)
        def _(step):
            forward(step)
            unit(step)

        l_copy(0, 16).wait_recv()

    multiply(z, lax.rem(z + 16, NZ))

    sib_copies = [remote(acc.at[h, :, 1 - c], sib.at[h], sib_send.at[h], sib_recv.at[h], sibling) for h in range(2)]
    for copy in sib_copies:
        copy.start()

    def x_copy(h, q):
        there = lax.rem(x + q, NX)
        return remote(acc.at[h, there, c], xin.at[q - 1, h], x_send.at[h, q - 1], x_recv.at[h, q - 1], at_x(q))

    for h in range(2):
        sib_copies[h].wait()
        for q in (2, 1, 3):
            there = lax.rem(x + q, NX)
            acc[h, there, c] = acc[h, there, c] + sib[h, there]
            x_copy(h, q).start()

    def yo_copy(h, q, src_y):
        return remote(
            red.at[h, :, 128 * q:128 * q + 128], fin.at[src_y, h], yo_send.at[h, q - 1], yo_recv.at[h, q - 1], at_y(q)
        )

    for h in range(2):
        mine = acc[h, x, c] + sib[h, x]
        for q in range(1, NX):
            x_copy(h, q).wait_recv()
            mine += xin[q - 1, h]
        red[h] = mine
        for q in (2, 1, 3):
            yo_copy(h, q, y).start()
        fin[y, h] = mine[:, 0:128]

    total = jnp.zeros((8, 128), F32)
    for n in far:
        far_copy(n, 0).wait_recv()
        total += mfin[n]

    lane8 = lax.broadcasted_iota(jnp.int32, (8, 128), 1)
    row8 = lax.broadcasted_iota(jnp.int32, (8, 128), 0)
    put = jnp.where((lane8 & (NA - 1)) == row8, 1.0, 0.0)
    by_l = lax.dot_general(total, put, DOT0, precision=lax.Precision.HIGHEST, preferred_element_type=F32)
    high = by_l.astype(BF16).astype(F32)
    lane32 = lax.broadcasted_iota(jnp.int32, (128, 32, 128), 2)
    row32 = lax.broadcasted_iota(jnp.int32, (128, 32, 128), 1)
    on_diagonal = (lane32 >> 2) == row32
    for n, term in enumerate((high, by_l - high)):
        wide = jnp.where(on_diagonal, jnp.broadcast_to(term[:, None, :], (128, 32, 128)), 0.0)
        spread[:, 128 * n:128 * n + 128] = wide.reshape(4096, 128).astype(BF16)
    both = jnp.dot(rt_hi[...], spread[...], preferred_element_type=F32)
    cycle = both[:, 0:128] + both[:, 128:256]
    cyc_ref[...] = cycle + jnp.dot(rt_lo[...], spread[:, 0:128], preferred_element_type=F32)

    for h in range(2):
        for q in range(1, NY):
            yo_copy(h, q, lax.rem(y + NY - q, NY)).wait_recv()
    lad_ref[...] = fin[...].reshape(O, 128)

    for q in range(1, NY):
        y_copy(q).wait_send()
        for h in range(2):
            yo_copy(h, q, y).wait_send()
    for copy in ig_copies:
        copy.wait_send()
    for h in range(2):
        for q in range(1, NX):
            x_copy(h, q).wait_send()

    @pl.when(c == 0)
    def _():
        for q in range(NY):
            yt_copy(q).wait_send()
        for q in range(1, NX):
            ms_copy(q).wait_send()
        for q in range(1, NY):
            my_copy(q).wait_send()
        for n in near:
            mz_copy(n).wait_send()
        for of in range(2):
            for n in far:
                far_copy(n, of).wait_send()

        @pl.loop(FAR[0], FAR[-1] + 1)
        def _(q):
            ma_copy(q).wait_send()

    @pl.when(c == 1)
    def _():
        for hand in hands:
            hand.wait_send()
        for stream in streams:
            @pl.loop(1, 16)
            def _(step):
                z_copy(stream, step).wait_send()
        for stream in last:
            z_copy(stream, 16).wait_send()
        for way in range(2):
            @pl.loop(1, 16)
            def _(step):
                l_copy(way, step).wait_send()
        l_copy(0, 16).wait_send()


def per_device(amplitudes, ladder_integral, tile_mask, left_factor, right_factor):
    own = amplitudes.reshape(NI * O, 16).T
    integral = ladder_integral.reshape(NY, NZ, 16, 128)
    left = jnp.transpose(left_factor, (1, 0, 2))
    vmem = pl.BlockSpec(memory_space=pltpu.VMEM)
    hbm = pl.BlockSpec(memory_space=pltpu.HBM)
    dma = pltpu.SemaphoreType.DMA
    n_near, n_far = (len(phase) for phase in Z_PHASES)
    ladder, cycle = pl.pallas_call(
        kernel,
        out_shape=(jax.ShapeDtypeStruct((O, 128), F32), jax.ShapeDtypeStruct((O, 128), F32)),
        in_specs=[hbm, hbm, pl.BlockSpec(memory_space=pltpu.SMEM), hbm, hbm],
        out_specs=(vmem, vmem),
        scratch_shapes=[
            pltpu.VMEM((16, NI * O), BF16),
            pltpu.VMEM((NY, NZ, 16, 128), BF16),
            pltpu.VMEM((2, 3, 128, 512), BF16),
            pltpu.VMEM((128, 32, O), F32),
            pltpu.VMEM((NY, 2, 16, HR), BF16),
            pltpu.VMEM((2, NY, NZ, 16, HR), BF16),
            pltpu.VMEM((2, NY, NZ, 16, HR), BF16),
            pltpu.VMEM((NY, NZ, 16, 512), BF16),
            pltpu.VMEM((2, NX, 2, KQ, 512), F32),
            pltpu.VMEM((2, NX, KQ, 512), F32),
            pltpu.VMEM((NX - 1, 2, KQ, 512), F32),
            pltpu.VMEM((2, KQ, 512), F32),
            pltpu.VMEM((NY, 2, KQ, 128), F32),
            pltpu.VMEM((4, 128, 128), F32),
            pltpu.VMEM((NZ, 2, 16, 128), BF16),
            pltpu.VMEM((NZ, 2, 16, 128), BF16),
            pltpu.VMEM((2, 512, 128), F32),
            pltpu.VMEM((2048, 128), F32),
            pltpu.VMEM((2, HR, 128), BF16),
            pltpu.VMEM((NS, 8, 128), F32),
            pltpu.VMEM((NS, 8, 128), F32),
            pltpu.VMEM((NX - 1, 2, 8, 128), F32),
            pltpu.VMEM((2, 8, 128), F32),
            pltpu.VMEM((NY - 1, 2, 8, 128), F32),
            pltpu.VMEM((2, 2, 8, 128), F32),
            pltpu.VMEM((n_near, 2, 8, 128), F32),
            pltpu.VMEM((n_far, 8, 128), F32),
            pltpu.VMEM((O, 4096), BF16),
            pltpu.VMEM((O, 4096), BF16),
            pltpu.VMEM((4096, 256), BF16),
            dma((4,)),
            pltpu.SemaphoreType.REGULAR,
            pltpu.SemaphoreType.REGULAR((3,)),
            dma((NY - 1,)), dma((NY - 1,)),
            dma((NY,)), dma((NY,)),
            dma((4,)), dma((4,)),
            dma((2, 2, 2, 17)), dma((2, 2, 2, 17)),
            dma((2, 17)), dma((2, 17)),
            dma((4,)), dma((4,)),
            dma((NZ - 1,)), dma((NZ - 1,)),
            dma((2,)), dma((2,)),
            dma((2, NX - 1)), dma((2, NX - 1)),
            dma((2, NY - 1)), dma((2, NY - 1)),
            dma((NX - 1,)), dma((NX - 1,)),
            dma((NY - 1,)), dma((NY - 1,)),
            dma((n_near,)), dma((n_near,)),
            dma((n_far, 2)), dma((n_far,)),
        ],
        compiler_params=pltpu.CompilerParams(
            collective_id=0, has_side_effects=True, vmem_limit_bytes=60 * 1024 * 1024
        ),
    )(own, integral, tile_mask.reshape(16), left, right_factor)
    return ladder + cycle


def solution(mesh):
    return jax.shard_map(
        per_device,
        mesh=mesh,
        in_specs=(
            P(None, "slab", "pair"),
            P("slab", "pair"),
            P("slab", "pair"),
            P(None, "pair", "slab"),
            P(None, "pair", None),
        ),
        out_specs=P("slab", "pair"),
        check_vma=False,
    )
```

time: 108 us -> 103 us (0.954)
  Pallas kernels: 106 us -> 101 us
  other arithmetic: 0 us -> 1.72 us
  local copies, waits for them, and re-layouts: 1.62 us -> 0 us
    pallas_call x1, Pallas kernels: 106 us -> 101 us  [per_device(): pl.pallas_call(kernel, out_shape=(jax.ShapeDtypeStruct((O, 128), F32), ja...]
    add x0 -> x1, other arithmetic: none -> 1.72 us  [per_device(): return ladder + cycle]
    unnamed x1 -> x0, local copies, waits for them, and re-layouts: 1.62 us -> none
where the time goes in v4:
time: 103 us
  Pallas kernels  101 us (98%)
  other arithmetic  1.72 us (2%)
    pallas_call x1, Pallas kernels, per_device(): pl.pallas_call(kernel, out_shape=(jax.ShapeDtypeStruct((O, 128), F32), ja...  101 us

profile of v4, /device:TPU:1, one launch (start us, length us, event | category | flops | bytes accessed | tf_op | source)
XLA Modules:
  0.0 103.1 jit_solution(13874850449881899809)
XLA Ops:
  0.0 101.4 %shard_map.55 = (f32[384,128]{1,0:T(8,128)}, f32[384,128]{1,0:T(8,128)}) custom-call(bf16[16,3072]{1,0:T(8,128)(2,1)} %bitcast.8, bf16[4,32,16,128]{3,2,1,0:T(8,128)(2,1)} %bitcast.6, s32[16]{0:T(128)} %bitcast.9, bf16[3,128,512]{2,1,0:T(8,128)(2,1)} %bitcast.7, f32[128,32,384]{2,1,0:T(8,128)} %right_hbm.1), custom_call_target="tpu_custom_call" | custom-call | tf_op jit(solution)/shard_map/pallas_call | solution.py:555
  101.4 1.7 %add.3 = f32[384,128]{1,0:T(8,128)} add(f32[384,128]{1,0:T(8,128)} %get-tuple-element.7, f32[384,128]{1,0:T(8,128)} %get-tuple-element.8) | non-fusion elementwise | flops 49152 | bytes 589824 | tf_op jit(solution)/shard_map/add | solution.py:613

commit v5 on v4

--- a/solution.py
+++ b/solution.py
@@ -151,7 +151,7 @@
         piece = (ts, tg)[of].at[h, :, slot]
         return remote(piece, piece, z_send.at[way, of, h, step], z_recv.at[way, of, h, step], at_z(sign))
 
-    streams = [(way, of, h) for h in range(2) for of in range(2) for way in range(2)]
+    streams = [(way, of, h) for of in range(2) for h in range(2) for way in range(2)]
     last = [stream for stream in streams if stream[0] == stream[2]]
 
     def l_copy(way, step):
@@ -245,14 +245,17 @@
         rt_hi[:, where] = high
         rt_lo[:, where] = (wide - high.astype(F32)).astype(BF16)
 
-    def multiply(first, second):
-        rhs = jnp.concatenate([ig[:, first].reshape(64, 512), ig[:, second].reshape(64, 512)], axis=0)
+    def multiply(*slots):
+        rhs = jnp.concatenate([ig[:, slot].reshape(64, 512) for slot in slots], axis=0)
         for h in range(2):
-            lhs = jnp.concatenate([tg[h, :, first].reshape(64, HR), tg[h, :, second].reshape(64, HR)], axis=0)
+            lhs = jnp.concatenate([tg[h, :, slot].reshape(64, HR) for slot in slots], axis=0)
             acc[h] += lax.dot_general(lhs, rhs, DOT0, preferred_element_type=F32).reshape(NX, 2, KQ, 512)
 
+    def pair_at(distance):
+        return lax.rem(z + NZ - distance, NZ), lax.rem(z + distance, NZ)
+
     def unit(distance):
-        multiply(lax.rem(z + NZ - distance, NZ), lax.rem(z + distance, NZ))
+        multiply(*pair_at(distance))
 
     tsel[...] = jnp.zeros_like(tsel)
     lane = lax.broadcasted_iota(jnp.int32, (HR, 128), 1)
@@ -290,11 +293,12 @@
     @pl.when(c == 1)
     def _():
         def forward(step):
-            for stream in streams:
+            for n, stream in enumerate(streams):
                 z_copy(stream, step, True).wait_recv()
                 z_copy(stream, step + 1).start()
-            for way in range(2):
-                l_copy(way, step).start()
+                if n == 3:
+                    for way in range(2):
+                        l_copy(way, step).start()
 
         def splits(step):
             split(2 * step - 2)
@@ -319,8 +323,7 @@
         ig_complete()
 
         def units(step):
-            unit(2 * step - 15)
-            unit(2 * step - 14)
+            multiply(*pair_at(2 * step - 15), *pair_at(2 * step - 14))
 
         @pl.loop(8, NEAR)
         def _(step):
@@ -339,16 +342,18 @@
             forward(step)
             units(step)
 
-        for stream in streams:
+        for n, stream in enumerate(streams):
             z_copy(stream, 15, True).wait_recv()
             if stream in last:
                 z_copy(stream, 16).start()
-        for way in range(2):
-            l_copy(way, 15).start()
+            if n == 3:
+                for way in range(2):
+                    l_copy(way, 15).start()
         unit(15)
-        for stream in last:
+        for n, stream in enumerate(last):
             z_copy(stream, 16, True).wait_recv()
-        l_copy(0, 16).start()
+            if n == 1:
+                l_copy(0, 16).start()
 
     @pl.when(c == 0)
     def _():

time: 103 us -> 102 us (level)
    pallas_call x1, Pallas kernels: 101 us -> 100 us  [per_device(): pl.pallas_call(kernel, out_shape=(jax.ShapeDtypeStruct((O, 128), F32), ja...]
where the time goes in v5:
time: 102 us
  Pallas kernels  100 us (98%)
  other arithmetic  1.72 us (2%)
    pallas_call x1, Pallas kernels, per_device(): pl.pallas_call(kernel, out_shape=(jax.ShapeDtypeStruct((O, 128), F32), ja...  100 us

profile of v5, /device:TPU:1, one launch (start us, length us, event | category | flops | bytes accessed | tf_op | source)
XLA Modules:
  0.0 102.0 jit_solution(17480375918901578505)
XLA Ops:
  0.0 100.3 %shard_map.55 = (f32[384,128]{1,0:T(8,128)}, f32[384,128]{1,0:T(8,128)}) custom-call(bf16[16,3072]{1,0:T(8,128)(2,1)} %bitcast.8, bf16[4,32,16,128]{3,2,1,0:T(8,128)(2,1)} %bitcast.6, s32[16]{0:T(128)} %bitcast.9, bf16[3,128,512]{2,1,0:T(8,128)(2,1)} %bitcast.7, f32[128,32,384]{2,1,0:T(8,128)} %right_hbm.1), custom_call_target="tpu_custom_call" | custom-call | tf_op jit(solution)/shard_map/pallas_call | solution.py:560
  100.3 1.7 %add.3 = f32[384,128]{1,0:T(8,128)} add(f32[384,128]{1,0:T(8,128)} %get-tuple-element.7, f32[384,128]{1,0:T(8,128)} %get-tuple-element.8) | non-fusion elementwise | flops 49152 | bytes 589824 | tf_op jit(solution)/shard_map/add | solution.py:618
